TPU v7x, 512 devices: a whole 4x4x16 slice. The times are simulated.
512 devices in a mesh: space: 32 (over z, core), tm: 16 (over x, y).
Axes of the slice: x: 4, y: 4, z: 16, core: 2. Of those that a mesh axis runs over, the one named last changes fastest.
Arguments:
- recordings: bfloat16 [2, 3, 512, 32768], P(None, None, 'space', 'tm'), may hold values from -30 to 30
- owner: int32 [512, 1], P('space'), may hold values from 0 to 31; in each aligned block of 16 rows (0 to 15, 16 to 31, ...) at most 2 rows name the same one
- valid_range: int32 [512, 2], P('space'), may hold values from 0 to 32768, as said below
- bin_mask: int32 [512, 96], P('space'), may hold values 0 or 1
Outputs:
- adjoint: bfloat16 [3, 2048, 32768], P(None, 'space', 'tm')
Inputs may be any that keep to these rules, and one draw needn't show every extreme that they name: `owner`: among the 16 receivers listed on one index of space, no subdomain owns more than 2; some subdomain owns exactly 2 of them. `valid_range`: column 0 is below column 1 in every row.
All inputs are finite; a program needn't handle non-finite values. No bound on the sum of `bin_mask` on one device may be relied on, other than what follows from the above.
Results may differ from a plain program's by a relative error of at most 0.013.
Values may be sent and summed in bfloat16 or wider, within the bound.
A program may use at most 128 MiB of HBM per device.

v0:
```python
import math
import jax
import jax.numpy as jnp
from jax import lax
from jax.sharding import PartitionSpec as P

BINS = 96
HOP = 256
HALO = 1024
KERNEL = 2304
WATER = 0.1
EPSILON = 1e-06


def with_halo(block, sides, width):
    for axis, dim in sides:
        count = lax.axis_size(axis)
        forward = [(i, i + 1) for i in range(count - 1)]
        backward = [(target, source) for source, target in forward]
        low = lax.ppermute(
            lax.slice_in_dim(block, block.shape[dim] - width, None, axis=dim), axis, forward
        )
        high = lax.ppermute(lax.slice_in_dim(block, 0, width, axis=dim), axis, backward)
        block = jnp.concatenate([low, block, high], axis=dim)
    return block


def shifted(block, axis, distance):
    devices = range(lax.axis_size(axis))
    route = [(i - distance, i) for i in devices if i - distance in devices]
    return lax.ppermute(block, axis, route)


def cq_kernel(kern_len, bins):
    octave_bins = bins // 8
    index = jnp.arange(bins).astype(jnp.float32)
    freq = 0.25 * jnp.exp2((index - (bins - 1)) / octave_bins)
    quality = 1.0 / (2.0 ** (1.0 / octave_bins) - 1.0)
    support = jnp.minimum(quality / freq, float(kern_len))
    offset = jnp.arange(kern_len).astype(jnp.float32) - 0.5 * (kern_len - 1)
    ratio = offset[:, None] / support[None, :]
    window = jnp.where(jnp.abs(ratio) < 0.5, 0.5 + 0.5 * jnp.cos(2.0 * math.pi * ratio), 0.0)
    window = window / jnp.sqrt(jnp.sum(window * window, axis=0, keepdims=True))
    cycles = offset[:, None] * freq[None, :]
    phase = cycles - jnp.floor(cycles)
    table = jnp.concatenate(
        [window * jnp.cos(2.0 * math.pi * phase), -window * jnp.sin(2.0 * math.pi * phase)], axis=1
    )
    return table.astype(jnp.bfloat16)


def adjoint_of(syn_re, syn_im, obs_re, obs_im, weight):
    level = (
        WATER * jnp.mean(obs_re * obs_re + obs_im * obs_im, axis=(-2, -1), keepdims=True) + EPSILON
    )
    syn_norm = jnp.sqrt(syn_re * syn_re + syn_im * syn_im + level)
    obs_norm = jnp.sqrt(obs_re * obs_re + obs_im * obs_im + level)
    diff_re = weight * (syn_re / syn_norm - obs_re / obs_norm)
    diff_im = weight * (syn_im / syn_norm - obs_im / obs_norm)
    inner = (syn_re * diff_re + syn_im * diff_im) / (syn_norm * syn_norm * syn_norm)
    return (diff_re / syn_norm - syn_re * inner, diff_im / syn_norm - syn_im * inner)


def analyse(blocks, table, frames):
    taps = table.shape[0] // HOP
    unfolded = jnp.concatenate([blocks[..., tap : tap + frames, :] for tap in range(taps)], axis=-1)
    return jnp.einsum("...fh,hk->...fk", unfolded, table, preferred_element_type=jnp.float32)


def synthesise(coefs, table, frames):
    taps = table.shape[0] // HOP
    term = jnp.einsum("...fk,hk->...fh", coefs, table, preferred_element_type=jnp.float32)
    term = term.reshape(term.shape[:-1] + (taps, HOP))
    lead = len(term.shape) - 3
    ext = jnp.zeros(coefs.shape[:-2] + (frames + taps - 1, HOP), jnp.float32)
    for tap in range(taps):
        widths = [(0, 0)] * lead + [(tap, taps - 1 - tap), (0, 0)]
        ext = ext + jnp.pad(term[..., tap, :], widths)
    return ext


def frame_weight(ranges, masks, frames_all):
    centers = jnp.arange(frames_all, dtype=jnp.int32) * HOP + HOP // 2
    inside = (ranges[:, 0:1] <= centers[None, :]) & (centers[None, :] < ranges[:, 1:2])
    return inside.astype(jnp.float32)[:, :, None] * masks.astype(jnp.float32)[:, None, :]


def misfit(coefs, weight):
    adj_re, adj_im = adjoint_of(
        coefs[0, ..., :BINS],
        coefs[0, ..., BINS:],
        coefs[1, ..., :BINS],
        coefs[1, ..., BINS:],
        weight,
    )
    joined = jnp.concatenate([adj_re, adj_im], axis=-1)
    return joined.reshape(joined.shape[:2] + (joined.shape[2] * joined.shape[3],)).astype(
        jnp.bfloat16
    )


def on_device(recordings, owner, valid_range, bin_mask):
    table = cq_kernel(KERNEL, BINS)
    margin = HALO // HOP
    width = 2 * BINS
    groups = lax.axis_size("tm")
    comps = recordings.shape[1]
    rec_dev = recordings.shape[2]
    samples_dev = recordings.shape[3]
    frames_dev = samples_dev // HOP
    rec_group = rec_dev // groups
    first_row = lax.axis_index("tm") * rec_group
    ranges = lax.dynamic_slice_in_dim(valid_range, first_row, rec_group, 0)
    masks = lax.dynamic_slice_in_dim(bin_mask, first_row, rec_group, 0)
    extended = with_halo(recordings, (("tm", 3),), HALO)
    blocks = extended.reshape(2, comps, rec_dev, frames_dev + 2 * margin, HOP)
    coefs = analyse(blocks, table, frames_dev)
    packed = coefs.astype(jnp.bfloat16).reshape(2, comps, rec_dev, frames_dev * width)
    weight = frame_weight(ranges, masks, frames_dev * groups)
    pieces = lax.all_to_all(packed, "tm", split_axis=2, concat_axis=3, tiled=True)
    items = pieces.shape[1]
    frames_all = pieces.shape[3] // width
    local_coefs = pieces.astype(jnp.float32).reshape(2, items, rec_group, frames_all, width)
    adjoint_local = misfit(local_coefs, weight)
    adjoint_back = lax.all_to_all(adjoint_local, "tm", split_axis=2, concat_axis=1, tiled=True)
    adjoint_frames = adjoint_back.reshape(comps, rec_dev, frames_dev, width)
    ext = synthesise(adjoint_frames, table, frames_dev)
    flat = ext.reshape(comps, rec_dev, (frames_dev + 2 * margin) * HOP)
    middle = flat[:, :, HALO : HALO + samples_dev]
    from_before = shifted(flat[:, :, HALO + samples_dev :].astype(jnp.bfloat16), "tm", 1).astype(
        jnp.float32
    )
    from_after = shifted(flat[:, :, :HALO].astype(jnp.bfloat16), "tm", -1).astype(jnp.float32)
    middle = middle.at[:, :, :HALO].add(from_before)
    middle = middle.at[:, :, samples_dev - HALO :].add(from_after)
    series = middle.astype(jnp.bfloat16)
    count = lax.axis_size("space")
    most = max(2, 3 * rec_dev // (2 * count))
    target = owner[:, 0]
    onehot = (target[:, None] == jnp.arange(count, dtype=jnp.int32)[None, :]).astype(jnp.int32)
    before = jnp.cumsum(onehot, axis=0) - onehot
    rank = jnp.sum(before * onehot, axis=1)
    slot = target * most + rank
    select = (jnp.arange(count * most, dtype=jnp.int32)[:, None] == slot[None, :]).astype(
        jnp.bfloat16
    )
    outgoing = jnp.einsum("sr,crt->cst", select, series, preferred_element_type=jnp.float32).astype(
        jnp.bfloat16
    )
    return lax.all_to_all(outgoing, "space", split_axis=1, concat_axis=1, tiled=True)


def solution(mesh):
    return jax.shard_map(
        on_device,
        mesh=mesh,
        in_specs=(
            P(None, None, "space", "tm"),
            P("space", None),
            P("space", None),
            P("space", None),
        ),
        out_specs=P(None, "space", "tm"),
        check_vma=False,
    )
```

profile of v0, /device:TPU:25, one launch (start us, length us, event | category | flops | bytes accessed | tf_op | source)
XLA Modules:
  0.0 347.0 jit_solution(11848009665123763137)
XLA Ops:
  0.0 1.1 fusion.24
  1.1 2.8 collective-permute-start
  3.9 2.5 collective-permute-start.1
  6.5 3.4 multiply_reduce_fusion
  9.9 6.7 %multiply_convert_fusion.3 = (bf16[2304,96]{0,1:T(8,128)(2,1)S(1)}, bf16[2304,96]{0,1:T(8,128)(2,1)S(1)}) fusion(f32[96]{0:T(128)S(1)} %get-tuple-element.51, f32[2304]{0:T(1024)S(1)} %convert_add_fusion.1, f32[96]{0:T(128)S(1)} %sqrt.38, f32[96]{0:T(128)S(1)} %get-tuple-element.50), kind=kLoop, calls=%fused_computation.19 | loop fusion | flops 3760128 | bytes 895104 | tf_op jit(solution)/shard_map/convert.7
  16.6 6.8 %multiply_convert_fusion.1 = (bf16[9,256,96]{1,2,0:T(8,128)(2,1)S(1)}, bf16[9,256,96]{1,2,0:T(8,128)(2,1)S(1)}) fusion(f32[96]{0:T(128)S(1)} %get-tuple-element.51, f32[9,256]{1,0:T(8,128)S(1)} %convert_add_fusion, f32[96]{0:T(128)S(1)} %sqrt.38, f32[96]{0:T(128)S(1)} %get-tuple-element.50), kind=kLoop, calls=%fused_computation.15 | loop fusion | flops 3760128 | bytes 895104 | tf_op jit(solution)/shard_map/convert.3
  23.5 0.7 fusion.19
  25.9 1.1 convolution_convert_fusion.1
  27.4 1.0 copy.61
  28.4 6.6 %all-to-all-start = ((bf16[2,3,16,1536]{3,0,1,2:T(2,128)(2,1)}), bf16[2,3,16,1536]{3,0,1,2:T(2,128)(2,1)S(1)}, u32[]{:S(2)}, u32[]{:S(2)}) async-start(bf16[2,3,16,1536]{3,0,1,2:T(2,128)(2,1)} %copy.61), calls=%async_computation | async-start | bytes 589824 | tf_op jit(solution)/shard_map/all_to_all | solution.py:120
  35.0 1.2 and_convert_fusion
  36.3 4.4 %all-to-all-done = bf16[2,3,16,1536]{3,0,1,2:T(2,128)(2,1)S(1)} async-done(((bf16[2,3,16,1536]{3,0,1,2:T(2,128)(2,1)}), bf16[2,3,16,1536]{3,0,1,2:T(2,128)(2,1)S(1)}, u32[]{:S(2)}, u32[]{:S(2)}) %all-to-all-start) | async-done | bytes 294944 | tf_op jit(solution)/shard_map/all_to_all | solution.py:120
  42.0 19.4 %copy.66 = bf16[3,1,24576]{0,1,2:T(2,128)(2,1)} copy(bf16[3,1,24576]{2,0,1:T(4,128)(2,1)S(1)} %convert_element_type.135) | data formatting | bytes 294912 | tf_op jit(solution)/shard_map/convert_element_type | solution.py:97
  61.9 134.9 %reduce.5 = bf16[24576,3]{1,0:T(8,128)(2,1)} reduce(bf16[24576,1,3]{2,1,0:T(2,128)(2,1)} %bitcast.152, bf16[]{:T(256)} %broadcast.341), dimensions={1}, to_apply=%bitcast.148.reduce_sub_computation | reduce | bytes 294914
  196.9 10.0 %reshape.529 = bf16[16,2,2304]{2,1,0:T(2,128)(2,1)} reshape(bf16[24576,3]{1,0:T(8,128)(2,1)} %reduce.5) | data formatting | bytes 294912
  206.9 5.5 %all-to-all-start.1 = ((bf16[16,2,2304]{2,1,0:T(2,128)(2,1)}), bf16[16,2,2304]{2,1,0:T(2,128)(2,1)S(1)}, u32[]{:S(2)}, u32[]{:S(2)}) async-start(bf16[16,2,2304]{2,1,0:T(2,128)(2,1)} %reshape.529), calls=%async_computation.1 | async-start | bytes 294912 | tf_op jit(solution)/shard_map/all_to_all | solution.py:125
  212.7 4.8 %all-to-all-done.1 = bf16[16,2,2304]{2,1,0:T(2,128)(2,1)S(1)} async-done(((bf16[16,2,2304]{2,1,0:T(2,128)(2,1)}), bf16[16,2,2304]{2,1,0:T(2,128)(2,1)S(1)}, u32[]{:S(2)}, u32[]{:S(2)}) %all-to-all-start.1) | async-done | bytes 147488 | tf_op jit(solution)/shard_map/all_to_all | solution.py:125
  217.5 14.4 %reshape.530 = bf16[24576,1,3]{2,1,0:T(2,128)(2,1)} reshape(bf16[16,2,2304]{2,1,0:T(2,128)(2,1)S(1)} %all-to-all-done.1) | data formatting | bytes 294912
  231.9 23.3 %copy.67 = bf16[3,1,24576]{2,0,1:T(4,128)(2,1)S(1)} copy(bf16[3,1,24576]{0,1,2:T(2,128)(2,1)} %bitcast.151) | data formatting | bytes 294912 | tf_op jit(solution)/shard_map/all_to_all | solution.py:125
  257.3 3.5 %collective-permute-start.2 = (bf16[3,16,1024]{2,1,0:T(8,128)(2,1)S(1)}, bf16[3,16,1024]{2,1,0:T(8,128)(2,1)S(1)}, u32[]{:S(2)}, u32[]{:S(2)}) collective-permute-start(bf16[3,16,1024]{2,1,0:T(8,128)(2,1)S(1)} %get-tuple-element.41), channel_id=1, source_target_pairs={{0,1},{1,2},{2,3},{3,4},{4,5},{5,6},{6,7},{7,8},{8,9},{9,10},{10,1... | collective-permute-start | bytes 294920 | tf_op jit(solution)/shard_map/ppermute | solution.py:31
  260.9 1.9 collective-permute-start.3
  262.8 5.5 %collective-permute-done.3 = bf16[3,16,1024]{2,1,0:T(8,128)(2,1)S(1)} collective-permute-done((bf16[3,16,1024]{2,1,0:T(8,128)(2,1)S(1)}, bf16[3,16,1024]{2,1,0:T(8,128)(2,1)S(1)}, u32[]{:S(2)}, u32[]{:S(2)}) %collective-permute-start.3) | collective-permute-done | bytes 98336 | tf_op jit(solution)/shard_map/ppermute | solution.py:31
  269.5 76.0 %all_to_all.23 = bf16[3,64,2048]{2,0,1:T(4,128)(2,1)S(1)} all-to-all(bf16[3,64,2048]{2,0,1:T(4,128)(2,1)S(1)} %copy.76), channel_id=1, replica_groups=mesh['space'=32,'tm'=16] {'space'}, dimensions={1} | all-to-all | bytes 1572864 | tf_op jit(solution)/shard_map/all_to_all | solution.py:150
  345.5 1.5 copy.77
  (52 shorter events, 7.5 us)
Async XLA Ops:
  0.0 23.4 %copy-start = (s32[16,2]{0,1:T(2,128)S(1)}, s32[16,2]{0,1:T(2,128)}, u32[]{:S(2)}) copy-start(s32[16,2]{0,1:T(2,128)} %param.10) | copy-start | bytes 388
  0.0 24.7 %copy-start.1 = (bf16[2,3,16,2048]{3,2,1,0:T(8,128)(2,1)S(1)}, bf16[2,3,16,2048]{3,2,1,0:T(8,128)(2,1)}, u32[]{:S(2)}) copy-start(bf16[2,3,16,2048]{3,2,1,0:T(8,128)(2,1)} %param.8) | copy-start | bytes 1179652
  1.1 23.6 %collective-permute-start = (bf16[2,3,16,1024]{3,2,1,0:T(8,128)(2,1)S(1)}, bf16[2,3,16,1024]{3,2,1,0:T(8,128)(2,1)S(1)}, u32[]{:S(2)}, u32[]{:S(2)}) collective-permute-start(bf16[2,3,16,1024]{3,2,1,0:T(8,128)(2,1)S(1)} %get-tuple-element.42), channel_id=1, source_target_pairs={{0,1},{1,2},{2,3},{3,4},{4,5},{5,6},{6,7},{7,8},{8,9},{9,10},{10,1... | collective-permute-start | bytes 589832 | tf_op jit(solution)/shard_map/ppermute | solution.py:20
  3.9 20.8 %collective-permute-start.1 = (bf16[2,3,16,1024]{3,2,1,0:T(8,128)(2,1)S(1)}, bf16[2,3,16,1024]{3,2,1,0:T(8,128)(2,1)S(1)}, u32[]{:S(2)}, u32[]{:S(2)}) collective-permute-start(bf16[2,3,16,1024]{3,2,1,0:T(8,128)(2,1)S(1)} %get-tuple-element.43), channel_id=1, source_target_pairs={{1,0},{2,1},{3,2},{4,3},{5,4},{6,5},{7,6},{8,7},{9,8},{10,9},{11,1... | collective-permute-start | bytes 589832 | tf_op jit(solution)/shard_map/ppermute | solution.py:23
  28.4 12.3 %all-to-all-start = ((bf16[2,3,16,1536]{3,0,1,2:T(2,128)(2,1)}), bf16[2,3,16,1536]{3,0,1,2:T(2,128)(2,1)S(1)}, u32[]{:S(2)}, u32[]{:S(2)}) async-start(bf16[2,3,16,1536]{3,0,1,2:T(2,128)(2,1)} %copy.61), calls=%async_computation | async-start | bytes 589824 | tf_op jit(solution)/shard_map/all_to_all | solution.py:120
  196.9 15.5 %copy-start.2 = (s32[16,1]{0,1:T(1,128)S(1)}, s32[16,1]{0,1:T(1,128)}, u32[]{:S(2)}) copy-start(s32[16,1]{0,1:T(1,128)} %param.9) | copy-start | bytes 196
  206.9 10.6 %all-to-all-start.1 = ((bf16[16,2,2304]{2,1,0:T(2,128)(2,1)}), bf16[16,2,2304]{2,1,0:T(2,128)(2,1)S(1)}, u32[]{:S(2)}, u32[]{:S(2)}) async-start(bf16[16,2,2304]{2,1,0:T(2,128)(2,1)} %reshape.529), calls=%async_computation.1 | async-start | bytes 294912 | tf_op jit(solution)/shard_map/all_to_all | solution.py:125
  257.3 5.5 %collective-permute-start.2 = (bf16[3,16,1024]{2,1,0:T(8,128)(2,1)S(1)}, bf16[3,16,1024]{2,1,0:T(8,128)(2,1)S(1)}, u32[]{:S(2)}, u32[]{:S(2)}) collective-permute-start(bf16[3,16,1024]{2,1,0:T(8,128)(2,1)S(1)} %get-tuple-element.41), channel_id=1, source_target_pairs={{0,1},{1,2},{2,3},{3,4},{4,5},{5,6},{6,7},{7,8},{8,9},{9,10},{10,1... | collective-permute-start | bytes 294920 | tf_op jit(solution)/shard_map/ppermute | solution.py:31
  260.9 7.5 %collective-permute-start.3 = (bf16[3,16,1024]{2,1,0:T(8,128)(2,1)S(1)}, bf16[3,16,1024]{2,1,0:T(8,128)(2,1)S(1)}, u32[]{:S(2)}, u32[]{:S(2)}) collective-permute-start(bf16[3,16,1024]{2,1,0:T(8,128)(2,1)S(1)} %get-tuple-element.40), channel_id=1, source_target_pairs={{1,0},{2,1},{3,2},{4,3},{5,4},{6,5},{7,6},{8,7},{9,8},{10,9},{11,1... | collective-permute-start | bytes 294920 | tf_op jit(solution)/shard_map/ppermute | solution.py:31
where the time goes:
time: 348 us; the launch traced here: 347 us
  other arithmetic  156 us (45%)
  blocking collectives  76 us (22%)
  local copies, waits for them, and re-layouts  75.2 us (22%)
  starting transfers between devices  22.8 us (7%)
  waiting for transfers between devices  14.8 us (4%)
    unnamed x1, other arithmetic  135 us
    all_to_all x1, blocking collectives, on_device(): lax.all_to_all(outgoing, 'space', split_axis=1, concat_axis=1, tiled=True)  76 us
    unnamed x18, local copies, waits for them, and re-layouts  26 us
    all_to_all x1, local copies, waits for them, and re-layouts, on_device(): lax.all_to_all(adjoint_local, 'tm', split_axis=2, concat_axis=1, tiled=True)  23.3 us
    convert_element_type x2, local copies, waits for them, and re-layouts, misfit(): joined.reshape(joined.shape[:2] + (joined.shape[2] * joined.shape[3],))  19.7 us
    another operation x4, other arithmetic  13.9 us
  transfers between devices with their start and end apart: 6, of which 3 were waited for; matrix products, arithmetic and copies ran while one was open for 6% of the time, Pallas kernels for 0%

commit v1 on v0

--- a/solution.py
+++ b/solution.py
@@ -10,6 +10,29 @@
 KERNEL = 2304
 WATER = 0.1
 EPSILON = 1e-06
+
+
+def in_blocks(x, dim, size):
+    dims = x.shape
+    tiles = x.reshape(*dims[:dim], size, dims[dim] // size, *dims[dim + 1 :])
+    return jnp.moveaxis(tiles, dim, 0)
+
+
+def laid_out(blocks, dim):
+    shape = list(blocks.shape[1:])
+    shape[dim] *= blocks.shape[0]
+    return jnp.moveaxis(blocks, 0, dim).reshape(shape)
+
+
+def swapped_with_each(x, axis, split_dim, concat_dim):
+    devices, index = (lax.axis_size(axis), lax.axis_index(axis))
+    blocks = in_blocks(x, split_dim, devices)
+    outs = [blocks[index]]
+    for step in range(1, devices):
+        sent = blocks[index ^ step]
+        outs.append(lax.ppermute(sent, axis, [(i, i ^ step) for i in range(devices)]))
+    blocks = jnp.stack(outs)[index ^ jnp.arange(devices)]
+    return laid_out(blocks, concat_dim)
 
 
 def with_halo(block, sides, width):
@@ -122,7 +145,7 @@
     frames_all = pieces.shape[3] // width
     local_coefs = pieces.astype(jnp.float32).reshape(2, items, rec_group, frames_all, width)
     adjoint_local = misfit(local_coefs, weight)
-    adjoint_back = lax.all_to_all(adjoint_local, "tm", split_axis=2, concat_axis=1, tiled=True)
+    adjoint_back = swapped_with_each(adjoint_local, "tm", 2, 1)
     adjoint_frames = adjoint_back.reshape(comps, rec_dev, frames_dev, width)
     ext = synthesise(adjoint_frames, table, frames_dev)
     flat = ext.reshape(comps, rec_dev, (frames_dev + 2 * margin) * HOP)

time: 348 us -> 199 us (0.57)
  other arithmetic: 156 us -> 20.8 us
  local copies, waits for them, and re-layouts: 75.2 us -> 8.96 us
  starting transfers between devices: 22.8 us -> 73.1 us
    unnamed x1 -> x0, other arithmetic: 135 us -> none
    ppermute x0 -> x15, starting transfers between devices: none -> 55.9 us  [swapped_with_each(): lax.ppermute(sent, axis, [(i, i ^ step) for i in range(devices)])]
    unnamed x18 -> x45, local copies, waits for them, and re-layouts: 26 us -> 1.35 us
    all_to_all x1 -> x0, local copies, waits for them, and re-layouts: 23.3 us -> none  [on_device(): lax.all_to_all(adjoint_local, 'tm', split_axis=2, concat_axis=1, tiled=True)]
    convert_element_type x2 -> x1, local copies, waits for them, and re-layouts: 19.7 us -> 0.17 us  [misfit(): joined.reshape(joined.shape[:2] + (joined.shape[2] * joined.shape[3],))]
    all_to_all x1 -> x0, starting transfers between devices: 5.49 us -> none  [on_device(): lax.all_to_all(adjoint_local, 'tm', split_axis=2, concat_axis=1, tiled=True)]
    all_to_all x1 -> x0, waiting for transfers between devices: 4.83 us -> none  [on_device(): lax.all_to_all(adjoint_local, 'tm', split_axis=2, concat_axis=1, tiled=True)]
    ppermute x0 -> x15, waiting for transfers between devices: none -> 3.48 us  [swapped_with_each(): lax.ppermute(sent, axis, [(i, i ^ step) for i in range(devices)])]
  transfers between devices with their start and end apart: 6 -> 20, of which waited for: 3 -> 3; matrix products, arithmetic and copies ran while one was open for 6% -> 10% of each run, Pallas kernels for 0% -> 0%
where the time goes in v1:
time: 199 us; the launch traced here: 197 us
  blocking collectives  79.4 us (40%)
  starting transfers between devices  73.1 us (37%)
  other arithmetic  20.8 us (10%)
  waiting for transfers between devices  11.8 us (6%)
  local copies, waits for them, and re-layouts  8.96 us (5%)
  matrix products  2.22 us (1%)
    all_to_all x1, blocking collectives, on_device(): lax.all_to_all(outgoing, 'space', split_axis=1, concat_axis=1, tiled=True)  79.4 us
    ppermute x15, starting transfers between devices, swapped_with_each(): lax.ppermute(sent, axis, [(i, i ^ step) for i in range(devices)])  55.9 us
    another operation x4, other arithmetic  13.9 us
    all_to_all x1, starting transfers between devices, on_device(): lax.all_to_all(packed, 'tm', split_axis=2, concat_axis=3, tiled=True)  6.61 us
    ppermute x2, starting transfers between devices, shifted(): return lax.ppermute(block, axis, route)  5.28 us
    all_to_all x1, waiting for transfers between devices, on_device(): lax.all_to_all(packed, 'tm', split_axis=2, concat_axis=3, tiled=True)  4.26 us
    ppermute x2, waiting for transfers between devices, shifted(): return lax.ppermute(block, axis, route)  4.08 us
  transfers between devices with their start and end apart: 20, of which 3 were waited for; matrix products, arithmetic and copies ran while one was open for 10% of the time, Pallas kernels for 0%

profile of v1, /device:TPU:25, one launch (start us, length us, event | category | flops | bytes accessed | tf_op | source)
XLA Modules:
  0.0 197.1 jit_solution(11954985447455754521)
XLA Ops:
  1.1 2.8 %collective-permute-start = (bf16[2,3,16,1024]{3,2,1,0:T(8,128)(2,1)S(1)}, bf16[2,3,16,1024]{3,2,1,0:T(8,128)(2,1)S(1)}, u32[]{:S(2)}, u32[]{:S(2)}) collective-permute-start(bf16[2,3,16,1024]{3,2,1,0:T(8,128)(2,1)S(1)} %get-tuple-element.42), channel_id=1, source_target_pairs={{0,1},{1,2},{2,3},{3,4},{4,5},{5,6},{6,7},{7,8},{8,9},{9,10},{10,1... | collective-permute-start | bytes 589832 | tf_op jit(solution)/shard_map/ppermute | solution.py:43
  3.9 2.5 %collective-permute-start.1 = (bf16[2,3,16,1024]{3,2,1,0:T(8,128)(2,1)S(1)}, bf16[2,3,16,1024]{3,2,1,0:T(8,128)(2,1)S(1)}, u32[]{:S(2)}, u32[]{:S(2)}) collective-permute-start(bf16[2,3,16,1024]{3,2,1,0:T(8,128)(2,1)S(1)} %get-tuple-element.43), channel_id=1, source_target_pairs={{1,0},{2,1},{3,2},{4,3},{5,4},{6,5},{7,6},{8,7},{9,8},{10,9},{11,1... | collective-permute-start | bytes 589832 | tf_op jit(solution)/shard_map/ppermute | solution.py:46
  6.5 3.4 %multiply_reduce_fusion = f32[96]{0:T(128)S(1)} fusion(f32[96]{0:T(128)S(1)} %get-tuple-element.66, f32[2304]{0:T(1024)S(1)} %convert_add_fusion.1), kind=kLoop, calls=%fused_computation.21 | loop fusion | flops 1990560 | bytes 9984 | tf_op jit(solution)/shard_map/reduce_sum | solution.py:66
  10.6 6.6 %multiply_convert_fusion.3 = (bf16[2304,96]{0,1:T(8,128)(2,1)S(1)}, bf16[2304,96]{0,1:T(8,128)(2,1)S(1)}) fusion(f32[96]{0:T(128)S(1)} %get-tuple-element.67, f32[2304]{0:T(1024)S(1)} %convert_add_fusion.1, f32[96]{0:T(128)S(1)} %sqrt.38, f32[96]{0:T(128)S(1)} %get-tuple-element.66), kind=kLoop, calls=%fused_computation.20 | loop fusion | flops 3760128 | bytes 895104 | tf_op jit(solution)/shard_map/convert.7
  17.2 6.8 %multiply_convert_fusion.1 = (bf16[9,256,96]{1,2,0:T(8,128)(2,1)S(1)}, bf16[9,256,96]{1,2,0:T(8,128)(2,1)S(1)}) fusion(f32[96]{0:T(128)S(1)} %get-tuple-element.67, f32[9,256]{1,0:T(8,128)S(1)} %convert_add_fusion, f32[96]{0:T(128)S(1)} %sqrt.38, f32[96]{0:T(128)S(1)} %get-tuple-element.66), kind=kLoop, calls=%fused_computation.16 | loop fusion | flops 3760128 | bytes 895104 | tf_op jit(solution)/shard_map/convert.3
  28.8 6.6 %all-to-all-start = ((bf16[2,3,16,1536]{3,0,1,2:T(2,128)(2,1)}), bf16[2,3,16,1536]{3,0,1,2:T(2,128)(2,1)S(1)}, u32[]{:S(2)}, u32[]{:S(2)}) async-start(bf16[2,3,16,1536]{3,0,1,2:T(2,128)(2,1)} %copy.76), calls=%async_computation | async-start | bytes 589824 | tf_op jit(solution)/shard_map/all_to_all | solution.py:143
  36.8 4.3 %all-to-all-done = bf16[2,3,16,1536]{3,0,1,2:T(2,128)(2,1)S(1)} async-done(((bf16[2,3,16,1536]{3,0,1,2:T(2,128)(2,1)}), bf16[2,3,16,1536]{3,0,1,2:T(2,128)(2,1)S(1)}, u32[]{:S(2)}, u32[]{:S(2)}) %all-to-all-start) | async-done | bytes 294944 | tf_op jit(solution)/shard_map/all_to_all | solution.py:143
  42.7 2.9 %collective-permute-start.2 = (bf16[3,1,1536]{2,0,1:T(4,128)(2,1)S(1)}, bf16[3,1,1536]{2,0,1:T(4,128)(2,1)S(1)}, u32[]{:S(2)}, u32[]{:S(2)}) collective-permute-start(bf16[3,1,1536]{2,0,1:T(4,128)(2,1)S(1)} %bitcast.264), channel_id=1, source_target_pairs={{0,1},{1,0},{2,3},{3,2},{4,5},{5,4},{6,7},{7,6},{8,9},{9,8},{10,11... | collective-permute-start | bytes 27656 | tf_op jit(solution)/shard_map/ppermute | solution.py:33
  45.7 4.0 %collective-permute-start.3 = (bf16[3,1,1536]{2,0,1:T(4,128)(2,1)S(1)}, bf16[3,1,1536]{2,0,1:T(4,128)(2,1)S(1)}, u32[]{:S(2)}, u32[]{:S(2)}) collective-permute-start(bf16[3,1,1536]{2,0,1:T(4,128)(2,1)S(1)} %bitcast.263), channel_id=1, source_target_pairs={{0,2},{1,3},{2,0},{3,1},{4,6},{5,7},{6,4},{7,5},{8,10},{9,11},{10,... | collective-permute-start | bytes 27656 | tf_op jit(solution)/shard_map/ppermute | solution.py:33
  49.7 2.6 %collective-permute-start.4 = (bf16[3,1,1536]{2,0,1:T(4,128)(2,1)S(1)}, bf16[3,1,1536]{2,0,1:T(4,128)(2,1)S(1)}, u32[]{:S(2)}, u32[]{:S(2)}) collective-permute-start(bf16[3,1,1536]{2,0,1:T(4,128)(2,1)S(1)} %bitcast.262), channel_id=1, source_target_pairs={{0,3},{1,2},{2,1},{3,0},{4,7},{5,6},{6,5},{7,4},{8,11},{9,10},{10,... | collective-permute-start | bytes 27656 | tf_op jit(solution)/shard_map/ppermute | solution.py:33
  52.4 2.1 %collective-permute-start.5 = (bf16[3,1,1536]{2,0,1:T(4,128)(2,1)S(1)}, bf16[3,1,1536]{2,0,1:T(4,128)(2,1)S(1)}, u32[]{:S(2)}, u32[]{:S(2)}) collective-permute-start(bf16[3,1,1536]{2,0,1:T(4,128)(2,1)S(1)} %bitcast.261), channel_id=1, source_target_pairs={{0,4},{1,5},{2,6},{3,7},{4,0},{5,1},{6,2},{7,3},{8,12},{9,13},{10,... | collective-permute-start | bytes 27656 | tf_op jit(solution)/shard_map/ppermute | solution.py:33
  54.5 2.7 %collective-permute-start.6 = (bf16[3,1,1536]{2,0,1:T(4,128)(2,1)S(1)}, bf16[3,1,1536]{2,0,1:T(4,128)(2,1)S(1)}, u32[]{:S(2)}, u32[]{:S(2)}) collective-permute-start(bf16[3,1,1536]{2,0,1:T(4,128)(2,1)S(1)} %bitcast.260), channel_id=1, source_target_pairs={{0,5},{1,4},{2,7},{3,6},{4,1},{5,0},{6,3},{7,2},{8,13},{9,12},{10,... | collective-permute-start | bytes 27656 | tf_op jit(solution)/shard_map/ppermute | solution.py:33
  57.4 5.0 %collective-permute-start.7 = (bf16[3,1,1536]{2,0,1:T(4,128)(2,1)S(1)}, bf16[3,1,1536]{2,0,1:T(4,128)(2,1)S(1)}, u32[]{:S(2)}, u32[]{:S(2)}) collective-permute-start(bf16[3,1,1536]{2,0,1:T(4,128)(2,1)S(1)} %bitcast.259), channel_id=1, source_target_pairs={{0,6},{1,7},{2,4},{3,5},{4,2},{5,3},{6,0},{7,1},{8,14},{9,15},{10,... | collective-permute-start | bytes 27656 | tf_op jit(solution)/shard_map/ppermute | solution.py:33
  62.4 3.8 %collective-permute-start.8 = (bf16[3,1,1536]{2,0,1:T(4,128)(2,1)S(1)}, bf16[3,1,1536]{2,0,1:T(4,128)(2,1)S(1)}, u32[]{:S(2)}, u32[]{:S(2)}) collective-permute-start(bf16[3,1,1536]{2,0,1:T(4,128)(2,1)S(1)} %bitcast.258), channel_id=1, source_target_pairs={{0,7},{1,6},{2,5},{3,4},{4,3},{5,2},{6,1},{7,0},{8,15},{9,14},{10,... | collective-permute-start | bytes 27656 | tf_op jit(solution)/shard_map/ppermute | solution.py:33
  66.2 3.1 %collective-permute-start.9 = (bf16[3,1,1536]{2,0,1:T(4,128)(2,1)S(1)}, bf16[3,1,1536]{2,0,1:T(4,128)(2,1)S(1)}, u32[]{:S(2)}, u32[]{:S(2)}) collective-permute-start(bf16[3,1,1536]{2,0,1:T(4,128)(2,1)S(1)} %bitcast.257), channel_id=1, source_target_pairs={{0,8},{1,9},{2,10},{3,11},{4,12},{5,13},{6,14},{7,15},{8,0},{9,1},... | collective-permute-start | bytes 27656 | tf_op jit(solution)/shard_map/ppermute | solution.py:33
  71.4 7.3 %collective-permute-start.11 = (bf16[3,1,1536]{2,0,1:T(4,128)(2,1)S(1)}, bf16[3,1,1536]{2,0,1:T(4,128)(2,1)S(1)}, u32[]{:S(2)}, u32[]{:S(2)}) collective-permute-start(bf16[3,1,1536]{2,0,1:T(4,128)(2,1)S(1)} %bitcast.255), channel_id=1, source_target_pairs={{0,10},{1,11},{2,8},{3,9},{4,14},{5,15},{6,12},{7,13},{8,2},{9,3},... | collective-permute-start | bytes 27656 | tf_op jit(solution)/shard_map/ppermute | solution.py:33
  78.8 4.2 %collective-permute-start.12 = (bf16[3,1,1536]{2,0,1:T(4,128)(2,1)S(1)}, bf16[3,1,1536]{2,0,1:T(4,128)(2,1)S(1)}, u32[]{:S(2)}, u32[]{:S(2)}) collective-permute-start(bf16[3,1,1536]{2,0,1:T(4,128)(2,1)S(1)} %bitcast.254), channel_id=1, source_target_pairs={{0,11},{1,10},{2,9},{3,8},{4,15},{5,14},{6,13},{7,12},{8,3},{9,2},... | collective-permute-start | bytes 27656 | tf_op jit(solution)/shard_map/ppermute | solution.py:33
  83.0 2.5 %collective-permute-start.13 = (bf16[3,1,1536]{2,0,1:T(4,128)(2,1)S(1)}, bf16[3,1,1536]{2,0,1:T(4,128)(2,1)S(1)}, u32[]{:S(2)}, u32[]{:S(2)}) collective-permute-start(bf16[3,1,1536]{2,0,1:T(4,128)(2,1)S(1)} %bitcast.253), channel_id=1, source_target_pairs={{0,12},{1,13},{2,14},{3,15},{4,8},{5,9},{6,10},{7,11},{8,4},{9,5},... | collective-permute-start | bytes 27656 | tf_op jit(solution)/shard_map/ppermute | solution.py:33
  87.5 7.6 %collective-permute-start.15 = (bf16[3,1,1536]{2,0,1:T(4,128)(2,1)S(1)}, bf16[3,1,1536]{2,0,1:T(4,128)(2,1)S(1)}, u32[]{:S(2)}, u32[]{:S(2)}) collective-permute-start(bf16[3,1,1536]{2,0,1:T(4,128)(2,1)S(1)} %bitcast.251), channel_id=1, source_target_pairs={{0,14},{1,15},{2,12},{3,13},{4,10},{5,11},{6,8},{7,9},{8,6},{9,7},... | collective-permute-start | bytes 27656 | tf_op jit(solution)/shard_map/ppermute | solution.py:33
  95.1 4.2 %collective-permute-start.16 = (bf16[3,1,1536]{2,0,1:T(4,128)(2,1)S(1)}, bf16[3,1,1536]{2,0,1:T(4,128)(2,1)S(1)}, u32[]{:S(2)}, u32[]{:S(2)}) collective-permute-start(bf16[3,1,1536]{2,0,1:T(4,128)(2,1)S(1)} %bitcast.250), channel_id=1, source_target_pairs={{0,15},{1,14},{2,13},{3,12},{4,11},{5,10},{6,9},{7,8},{8,7},{9,6},... | collective-permute-start | bytes 27656 | tf_op jit(solution)/shard_map/ppermute | solution.py:33
  99.4 3.4 %collective-permute-done.16 = bf16[3,1,1536]{2,0,1:T(4,128)(2,1)S(1)} collective-permute-done((bf16[3,1,1536]{2,0,1:T(4,128)(2,1)S(1)}, bf16[3,1,1536]{2,0,1:T(4,128)(2,1)S(1)}, u32[]{:S(2)}, u32[]{:S(2)}) %collective-permute-start.16) | collective-permute-done | bytes 9248 | tf_op jit(solution)/shard_map/ppermute | solution.py:33
  107.6 3.4 %collective-permute-start.18 = (bf16[3,16,1024]{2,1,0:T(8,128)(2,1)S(1)}, bf16[3,16,1024]{2,1,0:T(8,128)(2,1)S(1)}, u32[]{:S(2)}, u32[]{:S(2)}) collective-permute-start(bf16[3,16,1024]{2,1,0:T(8,128)(2,1)S(1)} %get-tuple-element.40), channel_id=1, source_target_pairs={{1,0},{2,1},{3,2},{4,3},{5,4},{6,5},{7,6},{8,7},{9,8},{10,9},{11,1... | collective-permute-start | bytes 294920 | tf_op jit(solution)/shard_map/ppermute | solution.py:54
  111.0 4.1 %collective-permute-done.18 = bf16[3,16,1024]{2,1,0:T(8,128)(2,1)S(1)} collective-permute-done((bf16[3,16,1024]{2,1,0:T(8,128)(2,1)S(1)}, bf16[3,16,1024]{2,1,0:T(8,128)(2,1)S(1)}, u32[]{:S(2)}, u32[]{:S(2)}) %collective-permute-start.18) | collective-permute-done | bytes 98336 | tf_op jit(solution)/shard_map/ppermute | solution.py:54
  116.3 79.4 %all_to_all.14 = bf16[3,64,2048]{2,0,1:T(4,128)(2,1)S(1)} all-to-all(bf16[3,64,2048]{2,0,1:T(4,128)(2,1)S(1)} %copy.91), channel_id=1, replica_groups=mesh['space'=32,'tm'=16] {'space'}, dimensions={1} | all-to-all | bytes 1572864 | tf_op jit(solution)/shard_map/all_to_all | solution.py:173
  (110 shorter events, 20.9 us)
Async XLA Ops:
  0.0 9.9 %copy-start = (s32[16,2]{0,1:T(2,128)S(1)}, s32[16,2]{0,1:T(2,128)}, u32[]{:S(2)}) copy-start(s32[16,2]{0,1:T(2,128)} %param.10) | copy-start | bytes 388
  0.0 25.1 %copy-start.1 = (bf16[2,3,16,2048]{3,2,1,0:T(8,128)(2,1)S(1)}, bf16[2,3,16,2048]{3,2,1,0:T(8,128)(2,1)}, u32[]{:S(2)}) copy-start(bf16[2,3,16,2048]{3,2,1,0:T(8,128)(2,1)} %param.8) | copy-start | bytes 1179652
  0.0 24.1 %copy-start.2 = (s32[16,1]{0,1:T(1,128)S(1)}, s32[16,1]{0,1:T(1,128)}, u32[]{:S(2)}) copy-start(s32[16,1]{0,1:T(1,128)} %param.9) | copy-start | bytes 196
  1.1 24.0 %collective-permute-start = (bf16[2,3,16,1024]{3,2,1,0:T(8,128)(2,1)S(1)}, bf16[2,3,16,1024]{3,2,1,0:T(8,128)(2,1)S(1)}, u32[]{:S(2)}, u32[]{:S(2)}) collective-permute-start(bf16[2,3,16,1024]{3,2,1,0:T(8,128)(2,1)S(1)} %get-tuple-element.42), channel_id=1, source_target_pairs={{0,1},{1,2},{2,3},{3,4},{4,5},{5,6},{6,7},{7,8},{8,9},{9,10},{10,1... | collective-permute-start | bytes 589832 | tf_op jit(solution)/shard_map/ppermute | solution.py:43
  3.9 21.2 %collective-permute-start.1 = (bf16[2,3,16,1024]{3,2,1,0:T(8,128)(2,1)S(1)}, bf16[2,3,16,1024]{3,2,1,0:T(8,128)(2,1)S(1)}, u32[]{:S(2)}, u32[]{:S(2)}) collective-permute-start(bf16[2,3,16,1024]{3,2,1,0:T(8,128)(2,1)S(1)} %get-tuple-element.43), channel_id=1, source_target_pairs={{1,0},{2,1},{3,2},{4,3},{5,4},{6,5},{7,6},{8,7},{9,8},{10,9},{11,1... | collective-permute-start | bytes 589832 | tf_op jit(solution)/shard_map/ppermute | solution.py:46
  28.8 12.3 %all-to-all-start = ((bf16[2,3,16,1536]{3,0,1,2:T(2,128)(2,1)}), bf16[2,3,16,1536]{3,0,1,2:T(2,128)(2,1)S(1)}, u32[]{:S(2)}, u32[]{:S(2)}) async-start(bf16[2,3,16,1536]{3,0,1,2:T(2,128)(2,1)} %copy.76), calls=%async_computation | async-start | bytes 589824 | tf_op jit(solution)/shard_map/all_to_all | solution.py:143
  42.7 14.7 %collective-permute-start.2 = (bf16[3,1,1536]{2,0,1:T(4,128)(2,1)S(1)}, bf16[3,1,1536]{2,0,1:T(4,128)(2,1)S(1)}, u32[]{:S(2)}, u32[]{:S(2)}) collective-permute-start(bf16[3,1,1536]{2,0,1:T(4,128)(2,1)S(1)} %bitcast.264), channel_id=1, source_target_pairs={{0,1},{1,0},{2,3},{3,2},{4,5},{5,4},{6,7},{7,6},{8,9},{9,8},{10,11... | collective-permute-start | bytes 27656 | tf_op jit(solution)/shard_map/ppermute | solution.py:33
  45.7 16.7 %collective-permute-start.3 = (bf16[3,1,1536]{2,0,1:T(4,128)(2,1)S(1)}, bf16[3,1,1536]{2,0,1:T(4,128)(2,1)S(1)}, u32[]{:S(2)}, u32[]{:S(2)}) collective-permute-start(bf16[3,1,1536]{2,0,1:T(4,128)(2,1)S(1)} %bitcast.263), channel_id=1, source_target_pairs={{0,2},{1,3},{2,0},{3,1},{4,6},{5,7},{6,4},{7,5},{8,10},{9,11},{10,... | collective-permute-start | bytes 27656 | tf_op jit(solution)/shard_map/ppermute | solution.py:33
  49.7 16.5 %collective-permute-start.4 = (bf16[3,1,1536]{2,0,1:T(4,128)(2,1)S(1)}, bf16[3,1,1536]{2,0,1:T(4,128)(2,1)S(1)}, u32[]{:S(2)}, u32[]{:S(2)}) collective-permute-start(bf16[3,1,1536]{2,0,1:T(4,128)(2,1)S(1)} %bitcast.262), channel_id=1, source_target_pairs={{0,3},{1,2},{2,1},{3,0},{4,7},{5,6},{6,5},{7,4},{8,11},{9,10},{10,... | collective-permute-start | bytes 27656 | tf_op jit(solution)/shard_map/ppermute | solution.py:33
  52.4 17.0 %collective-permute-start.5 = (bf16[3,1,1536]{2,0,1:T(4,128)(2,1)S(1)}, bf16[3,1,1536]{2,0,1:T(4,128)(2,1)S(1)}, u32[]{:S(2)}, u32[]{:S(2)}) collective-permute-start(bf16[3,1,1536]{2,0,1:T(4,128)(2,1)S(1)} %bitcast.261), channel_id=1, source_target_pairs={{0,4},{1,5},{2,6},{3,7},{4,0},{5,1},{6,2},{7,3},{8,12},{9,13},{10,... | collective-permute-start | bytes 27656 | tf_op jit(solution)/shard_map/ppermute | solution.py:33
  54.5 16.9 %collective-permute-start.6 = (bf16[3,1,1536]{2,0,1:T(4,128)(2,1)S(1)}, bf16[3,1,1536]{2,0,1:T(4,128)(2,1)S(1)}, u32[]{:S(2)}, u32[]{:S(2)}) collective-permute-start(bf16[3,1,1536]{2,0,1:T(4,128)(2,1)S(1)} %bitcast.260), channel_id=1, source_target_pairs={{0,5},{1,4},{2,7},{3,6},{4,1},{5,0},{6,3},{7,2},{8,13},{9,12},{10,... | collective-permute-start | bytes 27656 | tf_op jit(solution)/shard_map/ppermute | solution.py:33
  57.4 21.4 %collective-permute-start.7 = (bf16[3,1,1536]{2,0,1:T(4,128)(2,1)S(1)}, bf16[3,1,1536]{2,0,1:T(4,128)(2,1)S(1)}, u32[]{:S(2)}, u32[]{:S(2)}) collective-permute-start(bf16[3,1,1536]{2,0,1:T(4,128)(2,1)S(1)} %bitcast.259), channel_id=1, source_target_pairs={{0,6},{1,7},{2,4},{3,5},{4,2},{5,3},{6,0},{7,1},{8,14},{9,15},{10,... | collective-permute-start | bytes 27656 | tf_op jit(solution)/shard_map/ppermute | solution.py:33
  62.4 20.6 %collective-permute-start.8 = (bf16[3,1,1536]{2,0,1:T(4,128)(2,1)S(1)}, bf16[3,1,1536]{2,0,1:T(4,128)(2,1)S(1)}, u32[]{:S(2)}, u32[]{:S(2)}) collective-permute-start(bf16[3,1,1536]{2,0,1:T(4,128)(2,1)S(1)} %bitcast.258), channel_id=1, source_target_pairs={{0,7},{1,6},{2,5},{3,4},{4,3},{5,2},{6,1},{7,0},{8,15},{9,14},{10,... | collective-permute-start | bytes 27656 | tf_op jit(solution)/shard_map/ppermute | solution.py:33
  66.2 19.3 %collective-permute-start.9 = (bf16[3,1,1536]{2,0,1:T(4,128)(2,1)S(1)}, bf16[3,1,1536]{2,0,1:T(4,128)(2,1)S(1)}, u32[]{:S(2)}, u32[]{:S(2)}) collective-permute-start(bf16[3,1,1536]{2,0,1:T(4,128)(2,1)S(1)} %bitcast.257), channel_id=1, source_target_pairs={{0,8},{1,9},{2,10},{3,11},{4,12},{5,13},{6,14},{7,15},{8,0},{9,1},... | collective-permute-start | bytes 27656 | tf_op jit(solution)/shard_map/ppermute | solution.py:33
  69.4 18.1 %collective-permute-start.10 = (bf16[3,1,1536]{2,0,1:T(4,128)(2,1)S(1)}, bf16[3,1,1536]{2,0,1:T(4,128)(2,1)S(1)}, u32[]{:S(2)}, u32[]{:S(2)}) collective-permute-start(bf16[3,1,1536]{2,0,1:T(4,128)(2,1)S(1)} %bitcast.256), channel_id=1, source_target_pairs={{0,9},{1,8},{2,11},{3,10},{4,13},{5,12},{6,15},{7,14},{8,1},{9,0},... | collective-permute-start | bytes 27656 | tf_op jit(solution)/shard_map/ppermute | solution.py:33
  71.4 23.7 %collective-permute-start.11 = (bf16[3,1,1536]{2,0,1:T(4,128)(2,1)S(1)}, bf16[3,1,1536]{2,0,1:T(4,128)(2,1)S(1)}, u32[]{:S(2)}, u32[]{:S(2)}) collective-permute-start(bf16[3,1,1536]{2,0,1:T(4,128)(2,1)S(1)} %bitcast.255), channel_id=1, source_target_pairs={{0,10},{1,11},{2,8},{3,9},{4,14},{5,15},{6,12},{7,13},{8,2},{9,3},... | collective-permute-start | bytes 27656 | tf_op jit(solution)/shard_map/ppermute | solution.py:33
  78.8 20.5 %collective-permute-start.12 = (bf16[3,1,1536]{2,0,1:T(4,128)(2,1)S(1)}, bf16[3,1,1536]{2,0,1:T(4,128)(2,1)S(1)}, u32[]{:S(2)}, u32[]{:S(2)}) collective-permute-start(bf16[3,1,1536]{2,0,1:T(4,128)(2,1)S(1)} %bitcast.254), channel_id=1, source_target_pairs={{0,11},{1,10},{2,9},{3,8},{4,15},{5,14},{6,13},{7,12},{8,3},{9,2},... | collective-permute-start | bytes 27656 | tf_op jit(solution)/shard_map/ppermute | solution.py:33
  83.0 16.3 %collective-permute-start.13 = (bf16[3,1,1536]{2,0,1:T(4,128)(2,1)S(1)}, bf16[3,1,1536]{2,0,1:T(4,128)(2,1)S(1)}, u32[]{:S(2)}, u32[]{:S(2)}) collective-permute-start(bf16[3,1,1536]{2,0,1:T(4,128)(2,1)S(1)} %bitcast.253), channel_id=1, source_target_pairs={{0,12},{1,13},{2,14},{3,15},{4,8},{5,9},{6,10},{7,11},{8,4},{9,5},... | collective-permute-start | bytes 27656 | tf_op jit(solution)/shard_map/ppermute | solution.py:33
  85.5 13.8 %collective-permute-start.14 = (bf16[3,1,1536]{2,0,1:T(4,128)(2,1)S(1)}, bf16[3,1,1536]{2,0,1:T(4,128)(2,1)S(1)}, u32[]{:S(2)}, u32[]{:S(2)}) collective-permute-start(bf16[3,1,1536]{2,0,1:T(4,128)(2,1)S(1)} %bitcast.252), channel_id=1, source_target_pairs={{0,13},{1,12},{2,15},{3,14},{4,9},{5,8},{6,11},{7,10},{8,5},{9,4},... | collective-permute-start | bytes 27656 | tf_op jit(solution)/shard_map/ppermute | solution.py:33
  87.5 11.9 %collective-permute-start.15 = (bf16[3,1,1536]{2,0,1:T(4,128)(2,1)S(1)}, bf16[3,1,1536]{2,0,1:T(4,128)(2,1)S(1)}, u32[]{:S(2)}, u32[]{:S(2)}) collective-permute-start(bf16[3,1,1536]{2,0,1:T(4,128)(2,1)S(1)} %bitcast.251), channel_id=1, source_target_pairs={{0,14},{1,15},{2,12},{3,13},{4,10},{5,11},{6,8},{7,9},{8,6},{9,7},... | collective-permute-start | bytes 27656 | tf_op jit(solution)/shard_map/ppermute | solution.py:33
  95.1 7.8 %collective-permute-start.16 = (bf16[3,1,1536]{2,0,1:T(4,128)(2,1)S(1)}, bf16[3,1,1536]{2,0,1:T(4,128)(2,1)S(1)}, u32[]{:S(2)}, u32[]{:S(2)}) collective-permute-start(bf16[3,1,1536]{2,0,1:T(4,128)(2,1)S(1)} %bitcast.250), channel_id=1, source_target_pairs={{0,15},{1,14},{2,13},{3,12},{4,11},{5,10},{6,9},{7,8},{8,7},{9,6},... | collective-permute-start | bytes 27656 | tf_op jit(solution)/shard_map/ppermute | solution.py:33
  105.7 5.4 %collective-permute-start.17 = (bf16[3,16,1024]{2,1,0:T(8,128)(2,1)S(1)}, bf16[3,16,1024]{2,1,0:T(8,128)(2,1)S(1)}, u32[]{:S(2)}, u32[]{:S(2)}) collective-permute-start(bf16[3,16,1024]{2,1,0:T(8,128)(2,1)S(1)} %get-tuple-element.41), channel_id=1, source_target_pairs={{0,1},{1,2},{2,3},{3,4},{4,5},{5,6},{6,7},{7,8},{8,9},{9,10},{10,1... | collective-permute-start | bytes 294920 | tf_op jit(solution)/shard_map/ppermute | solution.py:54
  107.6 7.5 %collective-permute-start.18 = (bf16[3,16,1024]{2,1,0:T(8,128)(2,1)S(1)}, bf16[3,16,1024]{2,1,0:T(8,128)(2,1)S(1)}, u32[]{:S(2)}, u32[]{:S(2)}) collective-permute-start(bf16[3,16,1024]{2,1,0:T(8,128)(2,1)S(1)} %get-tuple-element.40), channel_id=1, source_target_pairs={{1,0},{2,1},{3,2},{4,3},{5,4},{6,5},{7,6},{8,7},{9,8},{10,9},{11,1... | collective-permute-start | bytes 294920 | tf_op jit(solution)/shard_map/ppermute | solution.py:54
